TPU v7x, 512 devices: a whole 4x8x8 slice. The times are simulated.
512 devices in a mesh: seq: 128 (over z_lo, x, y, core), head: 4 (over z_hi).
Axes of the slice: x: 4, y: 8, z: 8 (z_hi: 4, z_lo: 2; z = z_hi * 2 + z_lo), core: 2. Of those that a mesh axis runs over, the one named last changes fastest.
Arguments:
- queries: bfloat16 [16384, 4096], P('seq', 'head'), may hold values from -6 to 6
- key_rows: bfloat16 [16384, 4096], P('seq', 'head'), may hold values from -6 to 6
- values: bfloat16 [16384, 4096], P('seq', 'head'), may hold values from -11 to 11
- out_grad: bfloat16 [16384, 4096], P('seq', 'head'), may hold values from -11 to 11
- norm_gain: float32 [4096], P('head'), may hold values from 0.1 to 1.9
- head_levels: int32 [32, 7], P('head'), may hold values 0 or 1
Outputs:
- normed: bfloat16 [16384, 4096], P('seq', 'head')
- query_grad: bfloat16 [16384, 4096], P('seq', 'head')
- key_grad: bfloat16 [16384, 4096], P('seq', 'head')
- value_grad: bfloat16 [16384, 4096], P('seq', 'head')
- gain_grad: float32 [4096], P('head')
Inputs may be any that keep to these rules, and one draw needn't show every extreme that they name: head_levels[h, l] is 1 where head h reads the block 2**l blocks back.
All inputs are finite; a program needn't handle non-finite values.
Results may differ from a plain program's by a relative error of at most 0.018.
Values may be sent and summed in bfloat16 or wider, within the bound.
A program may use at most 64 MiB of HBM per device.

v0:
```python
import math
import jax
import jax.numpy as jnp
from jax import lax
from jax.sharding import PartitionSpec as P

D = 4096
HEAD_DIM = 128
EPSILON = 1e-06


def shifted(x, axis, by):
    devices = lax.axis_size(axis)
    pairs = [(i, i + by) for i in range(devices) if 0 <= i + by < devices]
    return lax.ppermute(x, axis, pairs)


def column_block(matrix, which_head, head_size):
    return lax.dynamic_slice_in_dim(matrix, which_head * head_size, head_size, 1)


def place_cols(buffer, portion, which_head, head_size):
    return lax.dynamic_update_slice_in_dim(buffer, portion, which_head * head_size, 1)


def contract_cols(left_side, right_side):
    return lax.dot_general(
        left_side, right_side, (((1,), (1,)), ((), ())), preferred_element_type=jnp.float32
    )


def contract_rows(left_side, right_side):
    return lax.dot_general(
        left_side, right_side, (((0,), (0,)), ((), ())), preferred_element_type=jnp.float32
    )


def body(queries, key_rows, values, out_grad, norm_gain, head_levels):
    f32 = jnp.float32
    bf16 = jnp.bfloat16
    tok_rows, row_width = queries.shape
    head_size = HEAD_DIM
    local_heads = row_width // head_size
    seq_devices = lax.axis_size("seq")
    level_count = seq_devices.bit_length() - 1
    block_index = lax.axis_index("seq")
    score_scale = 1.0 / math.sqrt(head_size)
    fetched = []
    for exponent in range(level_count):
        fetched.append(shifted((key_rows, values), "seq", 2**exponent))
    near_keys = jnp.concatenate([key_rows] + [received[0] for received in fetched], axis=0)
    near_values = jnp.concatenate([values] + [received[1] for received in fetched], axis=0)
    key_count = near_keys.shape[0]
    distance = 2 ** jnp.arange(level_count, dtype=jnp.int32)
    level_live = (head_levels == 1) & (block_index >= distance)[None, :]
    block_live = jnp.concatenate([jnp.ones((local_heads, 1), jnp.bool_), level_live], axis=1)
    key_block = jnp.arange(key_count, dtype=jnp.int32) // tok_rows
    key_place = jnp.arange(key_count, dtype=jnp.int32) % tok_rows
    row_place = jnp.arange(tok_rows, dtype=jnp.int32)
    causal = (key_block[None, :] > 0) | (key_place[None, :] <= row_place[:, None])
    block_hit = key_block[None, :] == jnp.arange(level_count + 1, dtype=jnp.int32)[:, None]

    def forward_head(which_head, buffers):
        context, weight_store, max_store, sum_store = buffers
        query_head = column_block(queries, which_head, head_size)
        key_head = column_block(near_keys, which_head, head_size)
        value_head = column_block(near_values, which_head, head_size)
        live_keys = jnp.any(block_hit & block_live[which_head][:, None], axis=0)
        scores = contract_cols(query_head, key_head) * score_scale
        scores = jnp.where(causal & live_keys[None, :], scores, -jnp.inf)
        row_max = jnp.max(scores, axis=1)
        raw_weights = jnp.exp(scores - row_max[:, None])
        row_sum = jnp.sum(raw_weights, axis=1)
        weights = (raw_weights / row_sum[:, None]).astype(bf16)
        head_out = jnp.dot(weights, value_head, preferred_element_type=f32).astype(bf16)
        return (
            place_cols(context, head_out, which_head, head_size),
            weight_store.at[which_head].set(weights),
            max_store.at[which_head].set(row_max),
            sum_store.at[which_head].set(row_sum),
        )

    start_buffers = (
        jnp.zeros((tok_rows, row_width), bf16),
        jnp.zeros((local_heads, tok_rows, key_count), bf16),
        jnp.zeros((local_heads, tok_rows), f32),
        jnp.zeros((local_heads, tok_rows), f32),
    )
    context, weight_store, max_store, sum_store = lax.fori_loop(
        0, local_heads, forward_head, start_buffers
    )
    context_f = context.astype(f32)
    squares = lax.psum(jnp.sum(context_f * context_f, axis=1), "head")
    inverse = lax.rsqrt(squares / D + EPSILON)
    normed = (context_f * inverse[:, None] * norm_gain[None, :]).astype(bf16)
    out_f = out_grad.astype(f32)
    scaled_grad = norm_gain[None, :] * out_f
    correction = lax.psum(jnp.sum(scaled_grad * context_f, axis=1), "head")
    context_grad = (
        inverse[:, None] * scaled_grad
        - (inverse * inverse * inverse * correction / D)[:, None] * context_f
    ).astype(bf16)
    gain_local = jnp.sum(out_f * context_f * inverse[:, None], axis=0)
    gain_grad = lax.psum(gain_local, "seq") / math.sqrt(seq_devices * tok_rows)
    out_dots = jnp.sum(
        (context_grad.astype(f32) * context_f).reshape(tok_rows, local_heads, head_size), axis=2
    ).T
    far_rows = key_count - tok_rows

    def backward_head(which_head, buffers):
        query_grad, key_near, value_near, key_far, value_far = buffers
        query_head = column_block(queries, which_head, head_size)
        key_head = column_block(near_keys, which_head, head_size)
        value_head = column_block(near_values, which_head, head_size)
        grad_head = column_block(context_grad, which_head, head_size)
        weights = weight_store[which_head]
        weight_grad = contract_cols(grad_head, value_head)
        score_grad = (
            weights.astype(f32) * (weight_grad - out_dots[which_head][:, None]) * score_scale
        ).astype(bf16)
        query_grad = place_cols(
            query_grad,
            jnp.dot(score_grad, key_head, preferred_element_type=f32).astype(bf16),
            which_head,
            head_size,
        )
        key_terms = contract_rows(score_grad, query_head)
        value_terms = contract_rows(weights, grad_head)
        key_near = place_cols(key_near, key_terms[:tok_rows], which_head, head_size)
        value_near = place_cols(value_near, value_terms[:tok_rows], which_head, head_size)
        key_far = place_cols(key_far, key_terms[tok_rows:].astype(bf16), which_head, head_size)
        value_far = place_cols(
            value_far, value_terms[tok_rows:].astype(bf16), which_head, head_size
        )
        return (query_grad, key_near, value_near, key_far, value_far)

    start_grads = (
        jnp.zeros((tok_rows, row_width), bf16),
        jnp.zeros((tok_rows, row_width), f32),
        jnp.zeros((tok_rows, row_width), f32),
        jnp.zeros((far_rows, row_width), bf16),
        jnp.zeros((far_rows, row_width), bf16),
    )
    query_grad, key_total, value_total, key_far, value_far = lax.fori_loop(
        0, local_heads, backward_head, start_grads
    )
    for exponent in range(level_count):
        first_row = exponent * tok_rows
        back_keys, back_values = shifted(
            (
                key_far[first_row : first_row + tok_rows],
                value_far[first_row : first_row + tok_rows],
            ),
            "seq",
            -(2**exponent),
        )
        key_total = key_total + back_keys.astype(f32)
        value_total = value_total + back_values.astype(f32)
    return (normed, query_grad, key_total.astype(bf16), value_total.astype(bf16), gain_grad)


def solution(mesh):
    placed = (
        P("seq", "head"),
        P("seq", "head"),
        P("seq", "head"),
        P("seq", "head"),
        P("head"),
        P("head", None),
    )
    return jax.shard_map(
        body,
        mesh=mesh,
        in_specs=placed,
        out_specs=(
            P("seq", "head"),
            P("seq", "head"),
            P("seq", "head"),
            P("seq", "head"),
            P("head"),
        ),
        check_vma=False,
    )
```

profile of v0, /device:TPU:78, one launch (start us, length us, event | category | flops | bytes accessed | tf_op | source)
XLA Modules:
  0.0 562.6 jit_solution(15485828811725810289)
XLA Ops:
  0.6 1.4 collective-permute-start.5
  2.1 1.3 collective-permute-start.4
  3.4 4.5 collective-permute-start.2
  7.9 4.7 collective-permute-start.1
  12.6 1.9 collective-permute-start
  14.5 1.7 constant_dynamic-update-slice_fusion.7
  18.0 5.1 collective-permute-done
  23.1 11.6 %collective-permute-start.3 = (bf16[128,1024]{1,0:T(8,128)(2,1)}, bf16[128,1024]{1,0:T(8,128)(2,1)S(1)}, u32[]{:S(2)}, u32[]{:S(2)}) collective-permute-start(bf16[128,1024]{1,0:T(8,128)(2,1)} %param.13), channel_id=1, source_target_pairs={{0,32},{4,36},{8,40},{12,44},{16,48},{20,52},{24,56},{28,60},{32,6... | collective-permute-start | bytes 786440 | tf_op jit(solution)/shard_map/ppermute | solution.py:15
  34.7 1.7 constant_dynamic-update-slice_fusion.6
  36.4 1.3 collective-permute-start.6
  38.4 1.3 collective-permute-start.12
  40.4 8.0 %collective-permute-done.3 = bf16[128,1024]{1,0:T(8,128)(2,1)S(1)} collective-permute-done((bf16[128,1024]{1,0:T(8,128)(2,1)}, bf16[128,1024]{1,0:T(8,128)(2,1)S(1)}, u32[]{:S(2)}, u32[]{:S(2)}) %collective-permute-start.3) | collective-permute-done | bytes 262176 | tf_op jit(solution)/shard_map/ppermute | solution.py:15
  48.4 1.3 collective-permute-start.11
  50.5 1.9 collective-permute-start.7
  53.1 4.5 collective-permute-start.8
  58.4 2.4 collective-permute-start.9
  61.4 1.9 collective-permute-start.10
  63.4 12.0 %collective-permute-done.8 = bf16[128,1024]{1,0:T(8,128)(2,1)S(1)} collective-permute-done((bf16[128,1024]{1,0:T(8,128)(2,1)S(1)}, bf16[128,1024]{1,0:T(8,128)(2,1)S(1)}, u32[]{:S(2)}, u32[]{:S(2)}) %collective-permute-start.8) | collective-permute-done | bytes 262176 | tf_op jit(solution)/shard_map/ppermute | solution.py:15
  75.4 1.3 collective-permute-start.13
  76.7 11.6 %collective-permute-done.9 = bf16[128,1024]{1,0:T(8,128)(2,1)S(1)} collective-permute-done((bf16[128,1024]{1,0:T(8,128)(2,1)S(1)}, bf16[128,1024]{1,0:T(8,128)(2,1)S(1)}, u32[]{:S(2)}, u32[]{:S(2)}) %collective-permute-start.9) | collective-permute-done | bytes 262176 | tf_op jit(solution)/shard_map/ppermute | solution.py:15
  88.4 5.2 collective-permute-done.13
  93.7 1.3 copy-done.1
  95.3 36.2 %while.39 = (s32[]{:T(128)}, bf16[128,1024]{1,0:T(8,128)(2,1)S(1)}, bf16[8,128,1024]{2,1,0:T(8,128)(2,1)S(1)}, pred[8,8]{1,0:T(8,128)(4,1)S(1)}, bf16[128,1024]{...) while((s32[]{:T(128)}, bf16[128,1024]{1,0:T(8,128)(2,1)S(1)}, ...), condition=%wide.region_5.6_spmd.clone, body=%wide.region_0.5_spmd.clone.sunk | while | flops 69114640 | bytes 3228417 | solution.py:89
  96.2 1.3 fusion.101
  100.7 1.3 fusion.101
  105.2 1.3 fusion.101
  109.7 1.3 fusion.101
  114.3 1.3 fusion.101
  118.8 1.3 fusion.101
  123.3 1.3 fusion.101
  127.8 1.3 fusion.101
  131.7 16.8 %psum.21 = f32[128]{0:T(128)S(1)} all-reduce(f32[128]{0:T(128)S(1)} %fusion.40), channel_id=1, replica_groups=mesh['seq'=128,'head'=4] {'head'}, use_global_device_ids=true, to_apply=%region_7.8 | all-reduce | flops 128 | bytes 1024 | tf_op jit(solution)/shard_map/psum | solution.py:93
  148.6 9.2 %psum.22 = f32[128]{0:T(128)S(1)} all-reduce(f32[128]{0:T(128)S(1)} %get-tuple-element.443), channel_id=1, replica_groups=mesh['seq'=128,'head'=4] {'head'}, use_global_device_ids=true, to_apply=%region_9.10 | all-reduce | flops 128 | bytes 1024 | tf_op jit(solution)/shard_map/psum | solution.py:98
  160.0 1.5 broadcast.287.clone
  161.4 1.5 broadcast.287
  162.9 41.5 %while.38 = (s32[]{:T(128)}, bf16[128,1024]{1,0:T(8,128)(2,1)}, f32[128,1024]{1,0:T(8,128)S(1)}, f32[128,1024]{1,0:T(8,128)S(1)}, bf16[896,1024]{1,0:T(8,128)(2,...) while((s32[]{:T(128)}, bf16[128,1024]{1,0:T(8,128)(2,1)}, ...), condition=%wide.region_12.13_spmd, body=%wide.region_11.12_spmd.sunk | while | flops 134889472 | bytes 4198627 | solution.py:144
  164.1 1.8 fusion.95
  169.3 1.8 fusion.95
  174.5 1.8 fusion.95
  179.7 1.8 fusion.95
  184.9 1.8 fusion.95
  190.1 1.8 fusion.95
  195.3 1.8 fusion.95
  200.5 1.8 fusion.95
  204.4 1.7 fusion.61
  206.2 1.9 collective-permute-start.21
  208.1 7.9 %collective-permute-start.27 = (bf16[128,1024]{1,0:T(8,128)(2,1)S(1)}, bf16[128,1024]{1,0:T(8,128)(2,1)S(1)}, u32[]{:S(2)}, u32[]{:S(2)}) collective-permute-start(bf16[128,1024]{1,0:T(8,128)(2,1)S(1)} %get-tuple-element.497), channel_id=1, source_target_pairs={{256,0},{260,4},{264,8},{268,12},{272,16},{276,20},{280,24},{284,2... | collective-permute-start | bytes 786440 | tf_op jit(solution)/shard_map/ppermute | solution.py:15
  216.0 1.3 collective-permute-start.26
  217.3 4.3 collective-permute-start.25
  221.6 1.9 collective-permute-start.24
  224.5 2.9 collective-permute-start.23
  227.4 5.6 collective-permute-start.22
  233.0 2.9 collective-permute-start.14
  235.9 3.2 collective-permute-start.20
  239.2 242.2 %psum.23 = f32[1024]{0:T(1024)S(1)} all-reduce(f32[1024]{0:T(1024)S(1)} %get-tuple-element.442), channel_id=1, replica_groups=mesh['seq'=128,'head'=4] {'seq'}, use_global_device_ids=true, to_apply=%region_14.15 | all-reduce | flops 1024 | bytes 8192 | tf_op jit(solution)/shard_map/psum | solution.py:104
  481.9 2.7 collective-permute-start.19
  484.7 44.5 %collective-permute-start.18 = (bf16[128,1024]{1,0:T(8,128)(2,1)S(1)}, bf16[128,1024]{1,0:T(8,128)(2,1)S(1)}, u32[]{:S(2)}, u32[]{:S(2)}) collective-permute-start(bf16[128,1024]{1,0:T(8,128)(2,1)S(1)} %get-tuple-element.506), channel_id=1, source_target_pairs={{64,0},{68,4},{72,8},{76,12},{80,16},{84,20},{88,24},{92,28},{96,3... | collective-permute-start | bytes 786440 | tf_op jit(solution)/shard_map/ppermute | solution.py:15
  529.2 1.9 collective-permute-start.17
  531.2 2.7 collective-permute-start.16
  533.9 7.6 %collective-permute-start.15 = (bf16[128,1024]{1,0:T(8,128)(2,1)S(1)}, bf16[128,1024]{1,0:T(8,128)(2,1)S(1)}, u32[]{:S(2)}, u32[]{:S(2)}) collective-permute-start(bf16[128,1024]{1,0:T(8,128)(2,1)S(1)} %get-tuple-element.509), channel_id=1, source_target_pairs={{8,0},{12,4},{16,8},{20,12},{24,16},{28,20},{32,24},{36,28},{40,32... | collective-permute-start | bytes 786440 | tf_op jit(solution)/shard_map/ppermute | solution.py:15
  541.5 2.5 add_convert_fusion
  544.6 6.6 %collective-permute-done.16 = bf16[128,1024]{1,0:T(8,128)(2,1)S(1)} collective-permute-done((bf16[128,1024]{1,0:T(8,128)(2,1)S(1)}, bf16[128,1024]{1,0:T(8,128)(2,1)S(1)}, u32[]{:S(2)}, u32[]{:S(2)}) %collective-permute-start.16) | collective-permute-done | bytes 262176 | tf_op jit(solution)/shard_map/ppermute | solution.py:15
  551.2 9.3 %collective-permute-done.15 = bf16[128,1024]{1,0:T(8,128)(2,1)S(1)} collective-permute-done((bf16[128,1024]{1,0:T(8,128)(2,1)S(1)}, bf16[128,1024]{1,0:T(8,128)(2,1)S(1)}, u32[]{:S(2)}, u32[]{:S(2)}) %collective-permute-start.15) | collective-permute-done | bytes 262176 | tf_op jit(solution)/shard_map/ppermute | solution.py:15
  560.6 2.1 add_convert_fusion.1
  (170 shorter events, 63.7 us)
Async XLA Ops:
  0.6 37.8 %copy-start.7 = (bf16[128,1024]{1,0:T(8,128)(2,1)S(1)}, bf16[128,1024]{1,0:T(8,128)(2,1)}, u32[]{:S(2)}) copy-start(bf16[128,1024]{1,0:T(8,128)(2,1)} %param.14) | copy-start | bytes 786436
  0.6 52.5 %collective-permute-start.5 = (bf16[128,1024]{1,0:T(8,128)(2,1)}, bf16[128,1024]{1,0:T(8,128)(2,1)S(1)}, u32[]{:S(2)}, u32[]{:S(2)}) collective-permute-start(bf16[128,1024]{1,0:T(8,128)(2,1)} %param.13), channel_id=1, source_target_pairs={{0,128},{4,132},{8,136},{12,140},{16,144},{20,148},{24,152},{28,15... | collective-permute-start | bytes 786440 | tf_op jit(solution)/shard_map/ppermute | solution.py:15
  2.1 48.4 %collective-permute-start.4 = (bf16[128,1024]{1,0:T(8,128)(2,1)}, bf16[128,1024]{1,0:T(8,128)(2,1)S(1)}, u32[]{:S(2)}, u32[]{:S(2)}) collective-permute-start(bf16[128,1024]{1,0:T(8,128)(2,1)} %param.13), channel_id=1, source_target_pairs={{0,64},{4,68},{8,72},{12,76},{16,80},{20,84},{24,88},{28,92},{32,9... | collective-permute-start | bytes 786440 | tf_op jit(solution)/shard_map/ppermute | solution.py:15
  3.4 35.0 %collective-permute-start.2 = (bf16[128,1024]{1,0:T(8,128)(2,1)}, bf16[128,1024]{1,0:T(8,128)(2,1)S(1)}, u32[]{:S(2)}, u32[]{:S(2)}) collective-permute-start(bf16[128,1024]{1,0:T(8,128)(2,1)} %param.13), channel_id=1, source_target_pairs={{0,16},{4,20},{8,24},{12,28},{16,32},{20,36},{24,40},{28,44},{32,4... | collective-permute-start | bytes 786440 | tf_op jit(solution)/shard_map/ppermute | solution.py:15
  7.9 28.5 %collective-permute-start.1 = (bf16[128,1024]{1,0:T(8,128)(2,1)}, bf16[128,1024]{1,0:T(8,128)(2,1)S(1)}, u32[]{:S(2)}, u32[]{:S(2)}) collective-permute-start(bf16[128,1024]{1,0:T(8,128)(2,1)} %param.13), channel_id=1, source_target_pairs={{0,8},{4,12},{8,16},{12,20},{16,24},{20,28},{24,32},{28,36},{32,40... | collective-permute-start | bytes 786440 | tf_op jit(solution)/shard_map/ppermute | solution.py:15
  12.6 10.5 %collective-permute-start = (bf16[128,1024]{1,0:T(8,128)(2,1)}, bf16[128,1024]{1,0:T(8,128)(2,1)}, u32[]{:S(2)}, u32[]{:S(2)}) collective-permute-start(bf16[128,1024]{1,0:T(8,128)(2,1)} %param.13), channel_id=1, source_target_pairs={{0,4},{4,8},{8,12},{12,16},{16,20},{20,24},{24,28},{28,32},{32,36}... | collective-permute-start | bytes 786440 | tf_op jit(solution)/shard_map/ppermute | solution.py:15
  23.1 25.3 %collective-permute-start.3 = (bf16[128,1024]{1,0:T(8,128)(2,1)}, bf16[128,1024]{1,0:T(8,128)(2,1)S(1)}, u32[]{:S(2)}, u32[]{:S(2)}) collective-permute-start(bf16[128,1024]{1,0:T(8,128)(2,1)} %param.13), channel_id=1, source_target_pairs={{0,32},{4,36},{8,40},{12,44},{16,48},{20,52},{24,56},{28,60},{32,6... | collective-permute-start | bytes 786440 | tf_op jit(solution)/shard_map/ppermute | solution.py:15
  36.4 22.0 %collective-permute-start.6 = (bf16[128,1024]{1,0:T(8,128)(2,1)}, bf16[128,1024]{1,0:T(8,128)(2,1)S(1)}, u32[]{:S(2)}, u32[]{:S(2)}) collective-permute-start(bf16[128,1024]{1,0:T(8,128)(2,1)} %param.13), channel_id=1, source_target_pairs={{0,256},{4,260},{8,264},{12,268},{16,272},{20,276},{24,280},{28,28... | collective-permute-start | bytes 786440 | tf_op jit(solution)/shard_map/ppermute | solution.py:15
  38.4 50.0 %collective-permute-start.12 = (bf16[128,1024]{1,0:T(8,128)(2,1)S(1)}, bf16[128,1024]{1,0:T(8,128)(2,1)S(1)}, u32[]{:S(2)}, u32[]{:S(2)}) collective-permute-start(bf16[128,1024]{1,0:T(8,128)(2,1)S(1)} %copy-done.7), channel_id=1, source_target_pairs={{0,128},{4,132},{8,136},{12,140},{16,144},{20,148},{24,152},{28,15... | collective-permute-start | bytes 786440 | tf_op jit(solution)/shard_map/ppermute | solution.py:15
  48.4 39.9 %collective-permute-start.11 = (bf16[128,1024]{1,0:T(8,128)(2,1)S(1)}, bf16[128,1024]{1,0:T(8,128)(2,1)S(1)}, u32[]{:S(2)}, u32[]{:S(2)}) collective-permute-start(bf16[128,1024]{1,0:T(8,128)(2,1)S(1)} %copy-done.7), channel_id=1, source_target_pairs={{0,64},{4,68},{8,72},{12,76},{16,80},{20,84},{24,88},{28,92},{32,9... | collective-permute-start | bytes 786440 | tf_op jit(solution)/shard_map/ppermute | solution.py:15
  50.5 11.0 %collective-permute-start.7 = (bf16[128,1024]{1,0:T(8,128)(2,1)S(1)}, bf16[128,1024]{1,0:T(8,128)(2,1)S(1)}, u32[]{:S(2)}, u32[]{:S(2)}) collective-permute-start(bf16[128,1024]{1,0:T(8,128)(2,1)S(1)} %copy-done.7), channel_id=1, source_target_pairs={{0,4},{4,8},{8,12},{12,16},{16,20},{20,24},{24,28},{28,32},{32,36}... | collective-permute-start | bytes 786440 | tf_op jit(solution)/shard_map/ppermute | solution.py:15
  53.1 22.3 %collective-permute-start.8 = (bf16[128,1024]{1,0:T(8,128)(2,1)S(1)}, bf16[128,1024]{1,0:T(8,128)(2,1)S(1)}, u32[]{:S(2)}, u32[]{:S(2)}) collective-permute-start(bf16[128,1024]{1,0:T(8,128)(2,1)S(1)} %copy-done.7), channel_id=1, source_target_pairs={{0,8},{4,12},{8,16},{12,20},{16,24},{20,28},{24,32},{28,36},{32,40... | collective-permute-start | bytes 786440 | tf_op jit(solution)/shard_map/ppermute | solution.py:15
  58.4 29.9 %collective-permute-start.9 = (bf16[128,1024]{1,0:T(8,128)(2,1)S(1)}, bf16[128,1024]{1,0:T(8,128)(2,1)S(1)}, u32[]{:S(2)}, u32[]{:S(2)}) collective-permute-start(bf16[128,1024]{1,0:T(8,128)(2,1)S(1)} %copy-done.7), channel_id=1, source_target_pairs={{0,16},{4,20},{8,24},{12,28},{16,32},{20,36},{24,40},{28,44},{32,4... | collective-permute-start | bytes 786440 | tf_op jit(solution)/shard_map/ppermute | solution.py:15
  61.4 26.9 %collective-permute-start.10 = (bf16[128,1024]{1,0:T(8,128)(2,1)S(1)}, bf16[128,1024]{1,0:T(8,128)(2,1)S(1)}, u32[]{:S(2)}, u32[]{:S(2)}) collective-permute-start(bf16[128,1024]{1,0:T(8,128)(2,1)S(1)} %copy-done.7), channel_id=1, source_target_pairs={{0,32},{4,36},{8,40},{12,44},{16,48},{20,52},{24,56},{28,60},{32,6... | collective-permute-start | bytes 786440 | tf_op jit(solution)/shard_map/ppermute | solution.py:15
  75.4 18.3 %collective-permute-start.13 = (bf16[128,1024]{1,0:T(8,128)(2,1)S(1)}, bf16[128,1024]{1,0:T(8,128)(2,1)S(1)}, u32[]{:S(2)}, u32[]{:S(2)}) collective-permute-start(bf16[128,1024]{1,0:T(8,128)(2,1)S(1)} %copy-done.7), channel_id=1, source_target_pairs={{0,256},{4,260},{8,264},{12,268},{16,272},{20,276},{24,280},{28,28... | collective-permute-start | bytes 786440 | tf_op jit(solution)/shard_map/ppermute | solution.py:15
  88.4 7.0 %copy-start.9 = (s32[3]{0:T(128)S(1)}, s32[3]{0:T(128)}, u32[]{:S(2)}) copy-start(s32[3]{0:T(128)} %constant.194.clone.2) | copy-start | bytes 40
  93.7 1.3 copy-start.1
  95.3 53.1 %copy-start.2 = (bf16[128,1024]{1,0:T(8,128)(2,1)S(1)}, bf16[128,1024]{1,0:T(8,128)(2,1)}, u32[]{:S(2)}) copy-start(bf16[128,1024]{1,0:T(8,128)(2,1)} %param.15) | copy-start | bytes 786436
  95.3 53.1 %copy-start.8 = (f32[1024]{0:T(1024)S(1)}, f32[1024]{0:T(1024)}, u32[]{:S(2)}) copy-start(f32[1024]{0:T(1024)} %param.16) | copy-start | bytes 12292
  204.4 19.1 %copy-start = (bf16[896,1024]{1,0:T(8,128)(2,1)S(1)}, bf16[896,1024]{1,0:T(8,128)(2,1)}, u32[]{:S(2)}) copy-start(bf16[896,1024]{1,0:T(8,128)(2,1)} %get-tuple-element.389) | copy-start | bytes 5505028
  206.2 18.3 %collective-permute-start.21 = (bf16[128,1024]{1,0:T(8,128)(2,1)S(1)}, bf16[128,1024]{1,0:T(8,128)(2,1)S(1)}, u32[]{:S(2)}, u32[]{:S(2)}) collective-permute-start(bf16[128,1024]{1,0:T(8,128)(2,1)S(1)} %get-tuple-element.496), channel_id=1, source_target_pairs={{4,0},{8,4},{12,8},{16,12},{20,16},{24,20},{28,24},{32,28},{36,32}... | collective-permute-start | bytes 786440 | tf_op jit(solution)/shard_map/ppermute | solution.py:15
  208.1 19.3 %collective-permute-start.27 = (bf16[128,1024]{1,0:T(8,128)(2,1)S(1)}, bf16[128,1024]{1,0:T(8,128)(2,1)S(1)}, u32[]{:S(2)}, u32[]{:S(2)}) collective-permute-start(bf16[128,1024]{1,0:T(8,128)(2,1)S(1)} %get-tuple-element.497), channel_id=1, source_target_pairs={{256,0},{260,4},{264,8},{268,12},{272,16},{276,20},{280,24},{284,2... | collective-permute-start | bytes 786440 | tf_op jit(solution)/shard_map/ppermute | solution.py:15
  216.0 17.0 %collective-permute-start.26 = (bf16[128,1024]{1,0:T(8,128)(2,1)S(1)}, bf16[128,1024]{1,0:T(8,128)(2,1)S(1)}, u32[]{:S(2)}, u32[]{:S(2)}) collective-permute-start(bf16[128,1024]{1,0:T(8,128)(2,1)S(1)} %get-tuple-element.498), channel_id=1, source_target_pairs={{128,0},{132,4},{136,8},{140,12},{144,16},{148,20},{152,24},{156,2... | collective-permute-start | bytes 786440 | tf_op jit(solution)/shard_map/ppermute | solution.py:15
  217.3 18.6 %collective-permute-start.25 = (bf16[128,1024]{1,0:T(8,128)(2,1)S(1)}, bf16[128,1024]{1,0:T(8,128)(2,1)S(1)}, u32[]{:S(2)}, u32[]{:S(2)}) collective-permute-start(bf16[128,1024]{1,0:T(8,128)(2,1)S(1)} %get-tuple-element.499), channel_id=1, source_target_pairs={{64,0},{68,4},{72,8},{76,12},{80,16},{84,20},{88,24},{92,28},{96,3... | collective-permute-start | bytes 786440 | tf_op jit(solution)/shard_map/ppermute | solution.py:15
  221.6 260.3 %collective-permute-start.24 = (bf16[128,1024]{1,0:T(8,128)(2,1)S(1)}, bf16[128,1024]{1,0:T(8,128)(2,1)}, u32[]{:S(2)}, u32[]{:S(2)}) collective-permute-start(bf16[128,1024]{1,0:T(8,128)(2,1)S(1)} %get-tuple-element.500), channel_id=1, source_target_pairs={{32,0},{36,4},{40,8},{44,12},{48,16},{52,20},{56,24},{60,28},{64,3... | collective-permute-start | bytes 786440 | tf_op jit(solution)/shard_map/ppermute | solution.py:15
  224.5 14.7 %copy-start.3 = (bf16[128,1024]{1,0:T(8,128)(2,1)}, bf16[128,1024]{1,0:T(8,128)(2,1)S(1)}, u32[]{:S(2)}) copy-start(bf16[128,1024]{1,0:T(8,128)(2,1)S(1)} %collective-permute-done.21) | copy-start | bytes 786436
  224.5 260.2 %collective-permute-start.23 = (bf16[128,1024]{1,0:T(8,128)(2,1)S(1)}, bf16[128,1024]{1,0:T(8,128)(2,1)}, u32[]{:S(2)}, u32[]{:S(2)}) collective-permute-start(bf16[128,1024]{1,0:T(8,128)(2,1)S(1)} %get-tuple-element.501), channel_id=1, source_target_pairs={{16,0},{20,4},{24,8},{28,12},{32,16},{36,20},{40,24},{44,28},{48,3... | collective-permute-start | bytes 786440 | tf_op jit(solution)/shard_map/ppermute | solution.py:15
  227.4 11.8 %copy-start.4 = (bf16[128,1024]{1,0:T(8,128)(2,1)}, bf16[128,1024]{1,0:T(8,128)(2,1)S(1)}, u32[]{:S(2)}) copy-start(bf16[128,1024]{1,0:T(8,128)(2,1)S(1)} %collective-permute-done.27) | copy-start | bytes 786436
  227.4 301.8 %collective-permute-start.22 = (bf16[128,1024]{1,0:T(8,128)(2,1)S(1)}, bf16[128,1024]{1,0:T(8,128)(2,1)}, u32[]{:S(2)}, u32[]{:S(2)}) collective-permute-start(bf16[128,1024]{1,0:T(8,128)(2,1)S(1)} %get-tuple-element.502), channel_id=1, source_target_pairs={{8,0},{12,4},{16,8},{20,12},{24,16},{28,20},{32,24},{36,28},{40,32... | collective-permute-start | bytes 786440 | tf_op jit(solution)/shard_map/ppermute | solution.py:15
  233.0 6.1 %copy-start.5 = (bf16[128,1024]{1,0:T(8,128)(2,1)}, bf16[128,1024]{1,0:T(8,128)(2,1)S(1)}, u32[]{:S(2)}) copy-start(bf16[128,1024]{1,0:T(8,128)(2,1)S(1)} %collective-permute-done.26) | copy-start | bytes 786436
  233.0 298.1 %collective-permute-start.14 = (bf16[128,1024]{1,0:T(8,128)(2,1)}, bf16[128,1024]{1,0:T(8,128)(2,1)}, u32[]{:S(2)}, u32[]{:S(2)}) collective-permute-start(bf16[128,1024]{1,0:T(8,128)(2,1)} %get-tuple-element.503), channel_id=1, source_target_pairs={{4,0},{8,4},{12,8},{16,12},{20,16},{24,20},{28,24},{32,28},{36,32}... | collective-permute-start | bytes 786440 | tf_op jit(solution)/shard_map/ppermute | solution.py:15
  235.9 3.2 copy-start.6
  235.9 298.0 %collective-permute-start.20 = (bf16[128,1024]{1,0:T(8,128)(2,1)S(1)}, bf16[128,1024]{1,0:T(8,128)(2,1)}, u32[]{:S(2)}, u32[]{:S(2)}) collective-permute-start(bf16[128,1024]{1,0:T(8,128)(2,1)S(1)} %get-tuple-element.504), channel_id=1, source_target_pairs={{256,0},{260,4},{264,8},{268,12},{272,16},{276,20},{280,24},{284,2... | collective-permute-start | bytes 786440 | tf_op jit(solution)/shard_map/ppermute | solution.py:15
  481.9 62.0 %collective-permute-start.19 = (bf16[128,1024]{1,0:T(8,128)(2,1)S(1)}, bf16[128,1024]{1,0:T(8,128)(2,1)S(1)}, u32[]{:S(2)}, u32[]{:S(2)}) collective-permute-start(bf16[128,1024]{1,0:T(8,128)(2,1)S(1)} %get-tuple-element.505), channel_id=1, source_target_pairs={{128,0},{132,4},{136,8},{140,12},{144,16},{148,20},{152,24},{156,2... | collective-permute-start | bytes 786440 | tf_op jit(solution)/shard_map/ppermute | solution.py:15
  484.7 59.3 %collective-permute-start.18 = (bf16[128,1024]{1,0:T(8,128)(2,1)S(1)}, bf16[128,1024]{1,0:T(8,128)(2,1)S(1)}, u32[]{:S(2)}, u32[]{:S(2)}) collective-permute-start(bf16[128,1024]{1,0:T(8,128)(2,1)S(1)} %get-tuple-element.506), channel_id=1, source_target_pairs={{64,0},{68,4},{72,8},{76,12},{80,16},{84,20},{88,24},{92,28},{96,3... | collective-permute-start | bytes 786440 | tf_op jit(solution)/shard_map/ppermute | solution.py:15
  529.2 15.4 %collective-permute-start.17 = (bf16[128,1024]{1,0:T(8,128)(2,1)S(1)}, bf16[128,1024]{1,0:T(8,128)(2,1)S(1)}, u32[]{:S(2)}, u32[]{:S(2)}) collective-permute-start(bf16[128,1024]{1,0:T(8,128)(2,1)S(1)} %get-tuple-element.507), channel_id=1, source_target_pairs={{32,0},{36,4},{40,8},{44,12},{48,16},{52,20},{56,24},{60,28},{64,3... | collective-permute-start | bytes 786440 | tf_op jit(solution)/shard_map/ppermute | solution.py:15
  531.2 20.1 %collective-permute-start.16 = (bf16[128,1024]{1,0:T(8,128)(2,1)S(1)}, bf16[128,1024]{1,0:T(8,128)(2,1)S(1)}, u32[]{:S(2)}, u32[]{:S(2)}) collective-permute-start(bf16[128,1024]{1,0:T(8,128)(2,1)S(1)} %get-tuple-element.508), channel_id=1, source_target_pairs={{16,0},{20,4},{24,8},{28,12},{32,16},{36,20},{40,24},{44,28},{48,3... | collective-permute-start | bytes 786440 | tf_op jit(solution)/shard_map/ppermute | solution.py:15
  533.9 26.7 %collective-permute-start.15 = (bf16[128,1024]{1,0:T(8,128)(2,1)S(1)}, bf16[128,1024]{1,0:T(8,128)(2,1)S(1)}, u32[]{:S(2)}, u32[]{:S(2)}) collective-permute-start(bf16[128,1024]{1,0:T(8,128)(2,1)S(1)} %get-tuple-element.509), channel_id=1, source_target_pairs={{8,0},{12,4},{16,8},{20,12},{24,16},{28,20},{32,24},{36,28},{40,32... | collective-permute-start | bytes 786440 | tf_op jit(solution)/shard_map/ppermute | solution.py:15
where the time goes:
time: 565 us; the launch traced here: 563 us
  blocking collectives  268 us (47%)
  starting transfers between devices  133 us (24%)
  waiting for transfers between devices  58.6 us (10%)
  matrix products  54.5 us (10%)
  local copies, waits for them, and re-layouts  24.5 us (4%)
  other arithmetic  22.6 us (4%)
    psum x1, blocking collectives, body(): gain_grad = lax.psum(gain_local, 'seq') / math.sqrt(seq_devices * tok_rows)  242 us
    ppermute x28, starting transfers between devices, shifted(): return lax.ppermute(x, axis, pairs)  133 us
    ppermute x28, waiting for transfers between devices, shifted(): return lax.ppermute(x, axis, pairs)  58.6 us
    dot_general x16, matrix products, contract_cols(): lax.dot_general(left_side, right_side, (((1,), (1,)), ((), ())), preferre...  19.9 us
    psum x1, blocking collectives, body(): squares = lax.psum(jnp.sum(context_f * context_f, axis=1), 'head')  16.8 us
    dot_general x8, matrix products, backward_head(): jnp.dot(score_grad, key_head, preferred_element_type=f32).astype(bf16)  14.4 us
  transfers between devices with their start and end apart: 28, of which 8 were waited for; matrix products, arithmetic and copies ran while one was open for 2% of the time, Pallas kernels for 0%

commit v1 on v0

--- a/solution.py
+++ b/solution.py
@@ -3,6 +3,7 @@
 import jax.numpy as jnp
 from jax import lax
 from jax.sharding import PartitionSpec as P
+from jax.lax import all_gather
 
 D = 4096
 HEAD_DIM = 128
@@ -36,6 +37,11 @@
 
 
 def body(queries, key_rows, values, out_grad, norm_gain, head_levels):
+
+    def advance_tracks(chunk):
+        a_next = all_gather(chunk, "seq")
+        return jnp.sum(a_next, 0)
+
     f32 = jnp.float32
     bf16 = jnp.bfloat16
     tok_rows, row_width = queries.shape
@@ -101,7 +107,7 @@
         - (inverse * inverse * inverse * correction / D)[:, None] * context_f
     ).astype(bf16)
     gain_local = jnp.sum(out_f * context_f * inverse[:, None], axis=0)
-    gain_grad = lax.psum(gain_local, "seq") / math.sqrt(seq_devices * tok_rows)
+    gain_grad = advance_tracks(gain_local) / math.sqrt(seq_devices * tok_rows)
     out_dots = jnp.sum(
         (context_grad.astype(f32) * context_f).reshape(tok_rows, local_heads, head_size), axis=2
     ).T

time: 565 us -> 450 us (0.80)
  the two profiles are of different devices: /device:TPU:78 before, /device:TPU:73 now
where the time goes in v1:
time: 450 us; the launch traced here: 448 us
  blocking collectives  187 us (42%)
  starting transfers between devices  89.5 us (20%)
  waiting for transfers between devices  66.8 us (15%)
  matrix products  54.5 us (12%)
  local copies, waits for them, and re-layouts  25.5 us (6%)
  other arithmetic  22.7 us (5%)
    all_gather x1, blocking collectives, advance_tracks(): a_next = all_gather(chunk, 'seq')  165 us
    ppermute x28, starting transfers between devices, shifted(): return lax.ppermute(x, axis, pairs)  89.5 us
    ppermute x28, waiting for transfers between devices, shifted(): return lax.ppermute(x, axis, pairs)  66.8 us
    dot_general x16, matrix products, contract_cols(): lax.dot_general(left_side, right_side, (((1,), (1,)), ((), ())), preferre...  19.9 us
    psum x1, blocking collectives, body(): squares = lax.psum(jnp.sum(context_f * context_f, axis=1), 'head')  14.7 us
    dot_general x8, matrix products, backward_head(): jnp.dot(score_grad, key_head, preferred_element_type=f32).astype(bf16)  14.4 us
    dot_general x16, matrix products, contract_rows(): lax.dot_general(left_side, right_side, (((0,), (0,)), ((), ())), preferre...  10.1 us
    dot_general x8, matrix products, forward_head(): jnp.dot(weights, value_head, preferred_element_type=f32).astype(bf16)  10.1 us
  transfers between devices with their start and end apart: 28, of which 6 were waited for; matrix products, arithmetic and copies ran while one was open for 3% of the time, Pallas kernels for 0%

profile of v1, /device:TPU:73, one launch (start us, length us, event | category | flops | bytes accessed | tf_op | source)
XLA Modules:
  0.0 447.6 jit_solution(14391629522307609574)
XLA Ops:
  0.6 4.8 %collective-permute-start.5 = (bf16[128,1024]{1,0:T(8,128)(2,1)}, bf16[128,1024]{1,0:T(8,128)(2,1)S(1)}, u32[]{:S(2)}, u32[]{:S(2)}) collective-permute-start(bf16[128,1024]{1,0:T(8,128)(2,1)} %param.13), channel_id=1, source_target_pairs={{0,128},{4,132},{8,136},{12,140},{16,144},{20,148},{24,152},{28,15... | collective-permute-start | bytes 786440 | tf_op jit(solution)/shard_map/ppermute | solution.py:16
  5.4 2.2 collective-permute-start.4
  7.7 4.2 collective-permute-start.2
  11.9 4.4 collective-permute-start.1
  16.3 4.0 collective-permute-start
  20.3 1.7 constant_dynamic-update-slice_fusion.7
  23.8 8.5 %collective-permute-done = bf16[128,1024]{1,0:T(8,128)(2,1)} collective-permute-done((bf16[128,1024]{1,0:T(8,128)(2,1)}, bf16[128,1024]{1,0:T(8,128)(2,1)}, u32[]{:S(2)}, u32[]{:S(2)}) %collective-permute-start) | collective-permute-done | bytes 262176 | tf_op jit(solution)/shard_map/ppermute | solution.py:16
  32.3 4.9 %collective-permute-start.3 = (bf16[128,1024]{1,0:T(8,128)(2,1)}, bf16[128,1024]{1,0:T(8,128)(2,1)S(1)}, u32[]{:S(2)}, u32[]{:S(2)}) collective-permute-start(bf16[128,1024]{1,0:T(8,128)(2,1)} %param.13), channel_id=1, source_target_pairs={{0,32},{4,36},{8,40},{12,44},{16,48},{20,52},{24,56},{28,60},{32,6... | collective-permute-start | bytes 786440 | tf_op jit(solution)/shard_map/ppermute | solution.py:16
  37.2 1.7 constant_dynamic-update-slice_fusion.6
  38.8 1.3 collective-permute-start.6
  40.9 1.9 collective-permute-start.12
  43.5 6.8 %collective-permute-done.3 = bf16[128,1024]{1,0:T(8,128)(2,1)S(1)} collective-permute-done((bf16[128,1024]{1,0:T(8,128)(2,1)}, bf16[128,1024]{1,0:T(8,128)(2,1)S(1)}, u32[]{:S(2)}, u32[]{:S(2)}) %collective-permute-start.3) | collective-permute-done | bytes 262176 | tf_op jit(solution)/shard_map/ppermute | solution.py:16
  50.3 1.9 collective-permute-start.11
  53.0 8.7 %collective-permute-start.7 = (bf16[128,1024]{1,0:T(8,128)(2,1)S(1)}, bf16[128,1024]{1,0:T(8,128)(2,1)S(1)}, u32[]{:S(2)}, u32[]{:S(2)}) collective-permute-start(bf16[128,1024]{1,0:T(8,128)(2,1)S(1)} %copy-done.7), channel_id=1, source_target_pairs={{0,4},{4,8},{8,12},{12,16},{16,20},{20,24},{24,28},{28,32},{32,36}... | collective-permute-start | bytes 786440 | tf_op jit(solution)/shard_map/ppermute | solution.py:16
  62.4 4.3 collective-permute-start.8
  67.4 1.9 collective-permute-start.9
  70.0 1.9 collective-permute-start.10
  72.0 3.5 collective-permute-done.8
  75.4 1.3 collective-permute-start.13
  76.8 23.5 %collective-permute-done.9 = bf16[128,1024]{1,0:T(8,128)(2,1)S(1)} collective-permute-done((bf16[128,1024]{1,0:T(8,128)(2,1)S(1)}, bf16[128,1024]{1,0:T(8,128)(2,1)S(1)}, u32[]{:S(2)}, u32[]{:S(2)}) %collective-permute-start.9) | collective-permute-done | bytes 262176 | tf_op jit(solution)/shard_map/ppermute | solution.py:16
  100.5 1.3 copy-done.1
  102.1 36.2 %while.39 = (s32[]{:T(128)}, bf16[128,1024]{1,0:T(8,128)(2,1)S(1)}, bf16[8,128,1024]{2,1,0:T(8,128)(2,1)S(1)}, pred[8,8]{1,0:T(8,128)(4,1)S(1)}, bf16[128,1024]{...) while((s32[]{:T(128)}, bf16[128,1024]{1,0:T(8,128)(2,1)S(1)}, ...), condition=%wide.region_5.6_spmd.clone, body=%wide.region_0.5_spmd.clone.sunk | while | flops 69114640 | bytes 3228417 | solution.py:95
  103.0 1.3 fusion.101
  107.5 1.3 fusion.101
  109.0 1.3 fusion.103
  112.0 1.3 fusion.101
  116.5 1.3 fusion.101
  121.1 1.3 fusion.101
  125.6 1.3 fusion.101
  130.1 1.3 fusion.101
  134.6 1.3 fusion.101
  138.5 14.7 %psum.14 = f32[128]{0:T(128)S(1)} all-reduce(f32[128]{0:T(128)S(1)} %fusion.40), channel_id=1, replica_groups=mesh['seq'=128,'head'=4] {'head'}, use_global_device_ids=true, to_apply=%region_7.8 | all-reduce | flops 128 | bytes 1024 | tf_op jit(solution)/shard_map/psum | solution.py:99
  153.4 7.4 %psum.15 = f32[128]{0:T(128)S(1)} all-reduce(f32[128]{0:T(128)S(1)} %get-tuple-element.443), channel_id=1, replica_groups=mesh['seq'=128,'head'=4] {'head'}, use_global_device_ids=true, to_apply=%region_9.10 | all-reduce | flops 128 | bytes 1024 | tf_op jit(solution)/shard_map/psum | solution.py:104
  163.0 1.5 broadcast.287.clone
  164.5 1.5 broadcast.287
  166.0 41.5 %while.38 = (s32[]{:T(128)}, bf16[128,1024]{1,0:T(8,128)(2,1)}, f32[128,1024]{1,0:T(8,128)S(1)}, f32[128,1024]{1,0:T(8,128)S(1)}, bf16[896,1024]{1,0:T(8,128)(2,...) while((s32[]{:T(128)}, bf16[128,1024]{1,0:T(8,128)(2,1)}, ...), condition=%wide.region_12.13_spmd, body=%wide.region_11.12_spmd.sunk | while | flops 134889472 | bytes 4198627 | solution.py:150
  167.2 1.8 fusion.95
  172.4 1.8 fusion.95
  177.6 1.8 fusion.95
  182.8 1.8 fusion.95
  188.0 1.8 fusion.95
  193.1 1.8 fusion.95
  198.3 1.8 fusion.95
  203.5 1.8 fusion.95
  207.5 2.5 fusion.61
  210.0 6.6 %collective-permute-start.21 = (bf16[128,1024]{1,0:T(8,128)(2,1)S(1)}, bf16[128,1024]{1,0:T(8,128)(2,1)S(1)}, u32[]{:S(2)}, u32[]{:S(2)}) collective-permute-start(bf16[128,1024]{1,0:T(8,128)(2,1)S(1)} %get-tuple-element.496), channel_id=1, source_target_pairs={{4,0},{8,4},{12,8},{16,12},{20,16},{24,20},{28,24},{32,28},{36,32}... | collective-permute-start | bytes 786440 | tf_op jit(solution)/shard_map/ppermute | solution.py:16
  216.6 1.3 collective-permute-start.27
  217.9 1.9 collective-permute-start.26
  219.8 2.7 collective-permute-start.25
  222.6 1.9 collective-permute-start.24
  225.5 4.2 collective-permute-start.23
  229.7 3.3 collective-permute-start.22
  233.0 2.8 collective-permute-start.14
  235.8 2.0 collective-permute-start.20
  237.9 164.8 %all-gather = f32[131072]{0:T(1024)S(1)} all-gather(f32[1024]{0:T(1024)S(1)} %get-tuple-element.442), channel_id=2, replica_groups=mesh['seq'=128,'head'=4] {'seq'}, dimensions={0}, use_global_device_ids=true | all-gather | bytes 528384 | tf_op jit(solution)/shard_map/all_gather | solution.py:42
  403.3 1.9 collective-permute-start.19
  405.3 1.9 collective-permute-start.18
  407.2 2.7 collective-permute-start.17
  410.0 5.3 %collective-permute-start.16 = (bf16[128,1024]{1,0:T(8,128)(2,1)S(1)}, bf16[128,1024]{1,0:T(8,128)(2,1)S(1)}, u32[]{:S(2)}, u32[]{:S(2)}) collective-permute-start(bf16[128,1024]{1,0:T(8,128)(2,1)S(1)} %get-tuple-element.508), channel_id=1, source_target_pairs={{16,0},{20,4},{24,8},{28,12},{32,16},{36,20},{40,24},{44,28},{48,3... | collective-permute-start | bytes 786440 | tf_op jit(solution)/shard_map/ppermute | solution.py:16
  415.3 3.2 collective-permute-start.15
  418.6 2.5 add_convert_fusion
  421.1 18.3 %collective-permute-done.16 = bf16[128,1024]{1,0:T(8,128)(2,1)S(1)} collective-permute-done((bf16[128,1024]{1,0:T(8,128)(2,1)S(1)}, bf16[128,1024]{1,0:T(8,128)(2,1)S(1)}, u32[]{:S(2)}, u32[]{:S(2)}) %collective-permute-start.16) | collective-permute-done | bytes 262176 | tf_op jit(solution)/shard_map/ppermute | solution.py:16
  439.4 6.2 %collective-permute-done.15 = bf16[128,1024]{1,0:T(8,128)(2,1)S(1)} collective-permute-done((bf16[128,1024]{1,0:T(8,128)(2,1)S(1)}, bf16[128,1024]{1,0:T(8,128)(2,1)S(1)}, u32[]{:S(2)}, u32[]{:S(2)}) %collective-permute-start.15) | collective-permute-done | bytes 262176 | tf_op jit(solution)/shard_map/ppermute | solution.py:16
  445.5 2.1 add_convert_fusion.1
  (172 shorter events, 62.0 us)
Async XLA Ops:
  0.6 40.2 %copy-start.7 = (bf16[128,1024]{1,0:T(8,128)(2,1)S(1)}, bf16[128,1024]{1,0:T(8,128)(2,1)}, u32[]{:S(2)}) copy-start(bf16[128,1024]{1,0:T(8,128)(2,1)} %param.14) | copy-start | bytes 786436
  0.6 61.7 %collective-permute-start.5 = (bf16[128,1024]{1,0:T(8,128)(2,1)}, bf16[128,1024]{1,0:T(8,128)(2,1)S(1)}, u32[]{:S(2)}, u32[]{:S(2)}) collective-permute-start(bf16[128,1024]{1,0:T(8,128)(2,1)} %param.13), channel_id=1, source_target_pairs={{0,128},{4,132},{8,136},{12,140},{16,144},{20,148},{24,152},{28,15... | collective-permute-start | bytes 786440 | tf_op jit(solution)/shard_map/ppermute | solution.py:16
  5.4 47.5 %collective-permute-start.4 = (bf16[128,1024]{1,0:T(8,128)(2,1)}, bf16[128,1024]{1,0:T(8,128)(2,1)S(1)}, u32[]{:S(2)}, u32[]{:S(2)}) collective-permute-start(bf16[128,1024]{1,0:T(8,128)(2,1)} %param.13), channel_id=1, source_target_pairs={{0,64},{4,68},{8,72},{12,76},{16,80},{20,84},{24,88},{28,92},{32,9... | collective-permute-start | bytes 786440 | tf_op jit(solution)/shard_map/ppermute | solution.py:16
  7.7 33.2 %collective-permute-start.2 = (bf16[128,1024]{1,0:T(8,128)(2,1)}, bf16[128,1024]{1,0:T(8,128)(2,1)S(1)}, u32[]{:S(2)}, u32[]{:S(2)}) collective-permute-start(bf16[128,1024]{1,0:T(8,128)(2,1)} %param.13), channel_id=1, source_target_pairs={{0,16},{4,20},{8,24},{12,28},{16,32},{20,36},{24,40},{28,44},{32,4... | collective-permute-start | bytes 786440 | tf_op jit(solution)/shard_map/ppermute | solution.py:16
  11.9 26.9 %collective-permute-start.1 = (bf16[128,1024]{1,0:T(8,128)(2,1)}, bf16[128,1024]{1,0:T(8,128)(2,1)S(1)}, u32[]{:S(2)}, u32[]{:S(2)}) collective-permute-start(bf16[128,1024]{1,0:T(8,128)(2,1)} %param.13), channel_id=1, source_target_pairs={{0,8},{4,12},{8,16},{12,20},{16,24},{20,28},{24,32},{28,36},{32,40... | collective-permute-start | bytes 786440 | tf_op jit(solution)/shard_map/ppermute | solution.py:16
  16.3 16.0 %collective-permute-start = (bf16[128,1024]{1,0:T(8,128)(2,1)}, bf16[128,1024]{1,0:T(8,128)(2,1)}, u32[]{:S(2)}, u32[]{:S(2)}) collective-permute-start(bf16[128,1024]{1,0:T(8,128)(2,1)} %param.13), channel_id=1, source_target_pairs={{0,4},{4,8},{8,12},{12,16},{16,20},{20,24},{24,28},{28,32},{32,36}... | collective-permute-start | bytes 786440 | tf_op jit(solution)/shard_map/ppermute | solution.py:16
  32.3 18.0 %collective-permute-start.3 = (bf16[128,1024]{1,0:T(8,128)(2,1)}, bf16[128,1024]{1,0:T(8,128)(2,1)S(1)}, u32[]{:S(2)}, u32[]{:S(2)}) collective-permute-start(bf16[128,1024]{1,0:T(8,128)(2,1)} %param.13), channel_id=1, source_target_pairs={{0,32},{4,36},{8,40},{12,44},{16,48},{20,52},{24,56},{28,60},{32,6... | collective-permute-start | bytes 786440 | tf_op jit(solution)/shard_map/ppermute | solution.py:16
  38.8 28.6 %collective-permute-start.6 = (bf16[128,1024]{1,0:T(8,128)(2,1)}, bf16[128,1024]{1,0:T(8,128)(2,1)S(1)}, u32[]{:S(2)}, u32[]{:S(2)}) collective-permute-start(bf16[128,1024]{1,0:T(8,128)(2,1)} %param.13), channel_id=1, source_target_pairs={{0,256},{4,260},{8,264},{12,268},{16,272},{20,276},{24,280},{28,28... | collective-permute-start | bytes 786440 | tf_op jit(solution)/shard_map/ppermute | solution.py:16
  40.9 59.5 %collective-permute-start.12 = (bf16[128,1024]{1,0:T(8,128)(2,1)S(1)}, bf16[128,1024]{1,0:T(8,128)(2,1)S(1)}, u32[]{:S(2)}, u32[]{:S(2)}) collective-permute-start(bf16[128,1024]{1,0:T(8,128)(2,1)S(1)} %copy-done.7), channel_id=1, source_target_pairs={{0,128},{4,132},{8,136},{12,140},{16,144},{20,148},{24,152},{28,15... | collective-permute-start | bytes 786440 | tf_op jit(solution)/shard_map/ppermute | solution.py:16
  50.3 50.0 %collective-permute-start.11 = (bf16[128,1024]{1,0:T(8,128)(2,1)S(1)}, bf16[128,1024]{1,0:T(8,128)(2,1)S(1)}, u32[]{:S(2)}, u32[]{:S(2)}) collective-permute-start(bf16[128,1024]{1,0:T(8,128)(2,1)S(1)} %copy-done.7), channel_id=1, source_target_pairs={{0,64},{4,68},{8,72},{12,76},{16,80},{20,84},{24,88},{28,92},{32,9... | collective-permute-start | bytes 786440 | tf_op jit(solution)/shard_map/ppermute | solution.py:16
  53.0 17.1 %collective-permute-start.7 = (bf16[128,1024]{1,0:T(8,128)(2,1)S(1)}, bf16[128,1024]{1,0:T(8,128)(2,1)S(1)}, u32[]{:S(2)}, u32[]{:S(2)}) collective-permute-start(bf16[128,1024]{1,0:T(8,128)(2,1)S(1)} %copy-done.7), channel_id=1, source_target_pairs={{0,4},{4,8},{8,12},{12,16},{16,20},{20,24},{24,28},{28,32},{32,36}... | collective-permute-start | bytes 786440 | tf_op jit(solution)/shard_map/ppermute | solution.py:16
  62.4 13.0 %collective-permute-start.8 = (bf16[128,1024]{1,0:T(8,128)(2,1)S(1)}, bf16[128,1024]{1,0:T(8,128)(2,1)S(1)}, u32[]{:S(2)}, u32[]{:S(2)}) collective-permute-start(bf16[128,1024]{1,0:T(8,128)(2,1)S(1)} %copy-done.7), channel_id=1, source_target_pairs={{0,8},{4,12},{8,16},{12,20},{16,24},{20,28},{24,32},{28,36},{32,40... | collective-permute-start | bytes 786440 | tf_op jit(solution)/shard_map/ppermute | solution.py:16
  67.4 32.9 %collective-permute-start.9 = (bf16[128,1024]{1,0:T(8,128)(2,1)S(1)}, bf16[128,1024]{1,0:T(8,128)(2,1)S(1)}, u32[]{:S(2)}, u32[]{:S(2)}) collective-permute-start(bf16[128,1024]{1,0:T(8,128)(2,1)S(1)} %copy-done.7), channel_id=1, source_target_pairs={{0,16},{4,20},{8,24},{12,28},{16,32},{20,36},{24,40},{28,44},{32,4... | collective-permute-start | bytes 786440 | tf_op jit(solution)/shard_map/ppermute | solution.py:16
  70.0 30.3 %collective-permute-start.10 = (bf16[128,1024]{1,0:T(8,128)(2,1)S(1)}, bf16[128,1024]{1,0:T(8,128)(2,1)S(1)}, u32[]{:S(2)}, u32[]{:S(2)}) collective-permute-start(bf16[128,1024]{1,0:T(8,128)(2,1)S(1)} %copy-done.7), channel_id=1, source_target_pairs={{0,32},{4,36},{8,40},{12,44},{16,48},{20,52},{24,56},{28,60},{32,6... | collective-permute-start | bytes 786440 | tf_op jit(solution)/shard_map/ppermute | solution.py:16
  75.4 25.0 %collective-permute-start.13 = (bf16[128,1024]{1,0:T(8,128)(2,1)S(1)}, bf16[128,1024]{1,0:T(8,128)(2,1)S(1)}, u32[]{:S(2)}, u32[]{:S(2)}) collective-permute-start(bf16[128,1024]{1,0:T(8,128)(2,1)S(1)} %copy-done.7), channel_id=1, source_target_pairs={{0,256},{4,260},{8,264},{12,268},{16,272},{20,276},{24,280},{28,28... | collective-permute-start | bytes 786440 | tf_op jit(solution)/shard_map/ppermute | solution.py:16
  100.4 1.8 copy-start.9
  100.5 1.3 copy-start.1
  102.1 51.1 %copy-start.2 = (bf16[128,1024]{1,0:T(8,128)(2,1)S(1)}, bf16[128,1024]{1,0:T(8,128)(2,1)}, u32[]{:S(2)}) copy-start(bf16[128,1024]{1,0:T(8,128)(2,1)} %param.15) | copy-start | bytes 786436
  102.1 51.1 %copy-start.8 = (f32[1024]{0:T(1024)S(1)}, f32[1024]{0:T(1024)}, u32[]{:S(2)}) copy-start(f32[1024]{0:T(1024)} %param.16) | copy-start | bytes 12292
  207.5 17.0 %copy-start = (bf16[896,1024]{1,0:T(8,128)(2,1)S(1)}, bf16[896,1024]{1,0:T(8,128)(2,1)}, u32[]{:S(2)}) copy-start(bf16[896,1024]{1,0:T(8,128)(2,1)} %get-tuple-element.389) | copy-start | bytes 5505028
  210.0 15.5 %collective-permute-start.21 = (bf16[128,1024]{1,0:T(8,128)(2,1)S(1)}, bf16[128,1024]{1,0:T(8,128)(2,1)S(1)}, u32[]{:S(2)}, u32[]{:S(2)}) collective-permute-start(bf16[128,1024]{1,0:T(8,128)(2,1)S(1)} %get-tuple-element.496), channel_id=1, source_target_pairs={{4,0},{8,4},{12,8},{16,12},{20,16},{24,20},{28,24},{32,28},{36,32}... | collective-permute-start | bytes 786440 | tf_op jit(solution)/shard_map/ppermute | solution.py:16
  216.6 13.1 %collective-permute-start.27 = (bf16[128,1024]{1,0:T(8,128)(2,1)S(1)}, bf16[128,1024]{1,0:T(8,128)(2,1)S(1)}, u32[]{:S(2)}, u32[]{:S(2)}) collective-permute-start(bf16[128,1024]{1,0:T(8,128)(2,1)S(1)} %get-tuple-element.497), channel_id=1, source_target_pairs={{256,0},{260,4},{264,8},{268,12},{272,16},{276,20},{280,24},{284,2... | collective-permute-start | bytes 786440 | tf_op jit(solution)/shard_map/ppermute | solution.py:16
  217.9 15.1 %collective-permute-start.26 = (bf16[128,1024]{1,0:T(8,128)(2,1)S(1)}, bf16[128,1024]{1,0:T(8,128)(2,1)S(1)}, u32[]{:S(2)}, u32[]{:S(2)}) collective-permute-start(bf16[128,1024]{1,0:T(8,128)(2,1)S(1)} %get-tuple-element.498), channel_id=1, source_target_pairs={{128,0},{132,4},{136,8},{140,12},{144,16},{148,20},{152,24},{156,2... | collective-permute-start | bytes 786440 | tf_op jit(solution)/shard_map/ppermute | solution.py:16
  219.8 16.0 %collective-permute-start.25 = (bf16[128,1024]{1,0:T(8,128)(2,1)S(1)}, bf16[128,1024]{1,0:T(8,128)(2,1)S(1)}, u32[]{:S(2)}, u32[]{:S(2)}) collective-permute-start(bf16[128,1024]{1,0:T(8,128)(2,1)S(1)} %get-tuple-element.499), channel_id=1, source_target_pairs={{64,0},{68,4},{72,8},{76,12},{80,16},{84,20},{88,24},{92,28},{96,3... | collective-permute-start | bytes 786440 | tf_op jit(solution)/shard_map/ppermute | solution.py:16
  222.6 180.8 %collective-permute-start.24 = (bf16[128,1024]{1,0:T(8,128)(2,1)}, bf16[128,1024]{1,0:T(8,128)(2,1)}, u32[]{:S(2)}, u32[]{:S(2)}) collective-permute-start(bf16[128,1024]{1,0:T(8,128)(2,1)} %get-tuple-element.500), channel_id=1, source_target_pairs={{32,0},{36,4},{40,8},{44,12},{48,16},{52,20},{56,24},{60,28},{64,3... | collective-permute-start | bytes 786440 | tf_op jit(solution)/shard_map/ppermute | solution.py:16
  225.5 12.3 %copy-start.3 = (bf16[128,1024]{1,0:T(8,128)(2,1)}, bf16[128,1024]{1,0:T(8,128)(2,1)S(1)}, u32[]{:S(2)}) copy-start(bf16[128,1024]{1,0:T(8,128)(2,1)S(1)} %collective-permute-done.21) | copy-start | bytes 786436
  225.5 179.8 %collective-permute-start.23 = (bf16[128,1024]{1,0:T(8,128)(2,1)}, bf16[128,1024]{1,0:T(8,128)(2,1)}, u32[]{:S(2)}, u32[]{:S(2)}) collective-permute-start(bf16[128,1024]{1,0:T(8,128)(2,1)} %get-tuple-element.501), channel_id=1, source_target_pairs={{16,0},{20,4},{24,8},{28,12},{32,16},{36,20},{40,24},{44,28},{48,3... | collective-permute-start | bytes 786440 | tf_op jit(solution)/shard_map/ppermute | solution.py:16
  229.7 8.1 %copy-start.4 = (bf16[128,1024]{1,0:T(8,128)(2,1)}, bf16[128,1024]{1,0:T(8,128)(2,1)S(1)}, u32[]{:S(2)}) copy-start(bf16[128,1024]{1,0:T(8,128)(2,1)S(1)} %collective-permute-done.27) | copy-start | bytes 786436
  229.7 177.5 %collective-permute-start.22 = (bf16[128,1024]{1,0:T(8,128)(2,1)}, bf16[128,1024]{1,0:T(8,128)(2,1)}, u32[]{:S(2)}, u32[]{:S(2)}) collective-permute-start(bf16[128,1024]{1,0:T(8,128)(2,1)} %get-tuple-element.502), channel_id=1, source_target_pairs={{8,0},{12,4},{16,8},{20,12},{24,16},{28,20},{32,24},{36,28},{40,32... | collective-permute-start | bytes 786440 | tf_op jit(solution)/shard_map/ppermute | solution.py:16
  233.0 4.8 %copy-start.5 = (bf16[128,1024]{1,0:T(8,128)(2,1)}, bf16[128,1024]{1,0:T(8,128)(2,1)S(1)}, u32[]{:S(2)}) copy-start(bf16[128,1024]{1,0:T(8,128)(2,1)S(1)} %collective-permute-done.26) | copy-start | bytes 786436
  233.0 176.9 %collective-permute-start.14 = (bf16[128,1024]{1,0:T(8,128)(2,1)}, bf16[128,1024]{1,0:T(8,128)(2,1)}, u32[]{:S(2)}, u32[]{:S(2)}) collective-permute-start(bf16[128,1024]{1,0:T(8,128)(2,1)} %get-tuple-element.503), channel_id=1, source_target_pairs={{4,0},{8,4},{12,8},{16,12},{20,16},{24,20},{28,24},{32,28},{36,32}... | collective-permute-start | bytes 786440 | tf_op jit(solution)/shard_map/ppermute | solution.py:16
  235.8 2.0 copy-start.6
  235.8 179.5 %collective-permute-start.20 = (bf16[128,1024]{1,0:T(8,128)(2,1)}, bf16[128,1024]{1,0:T(8,128)(2,1)}, u32[]{:S(2)}, u32[]{:S(2)}) collective-permute-start(bf16[128,1024]{1,0:T(8,128)(2,1)} %get-tuple-element.504), channel_id=1, source_target_pairs={{256,0},{260,4},{264,8},{268,12},{272,16},{276,20},{280,24},{284,2... | collective-permute-start | bytes 786440 | tf_op jit(solution)/shard_map/ppermute | solution.py:16
  403.3 17.7 %collective-permute-start.19 = (bf16[128,1024]{1,0:T(8,128)(2,1)S(1)}, bf16[128,1024]{1,0:T(8,128)(2,1)S(1)}, u32[]{:S(2)}, u32[]{:S(2)}) collective-permute-start(bf16[128,1024]{1,0:T(8,128)(2,1)S(1)} %get-tuple-element.505), channel_id=1, source_target_pairs={{128,0},{132,4},{136,8},{140,12},{144,16},{148,20},{152,24},{156,2... | collective-permute-start | bytes 786440 | tf_op jit(solution)/shard_map/ppermute | solution.py:16
  405.3 15.8 %collective-permute-start.18 = (bf16[128,1024]{1,0:T(8,128)(2,1)S(1)}, bf16[128,1024]{1,0:T(8,128)(2,1)S(1)}, u32[]{:S(2)}, u32[]{:S(2)}) collective-permute-start(bf16[128,1024]{1,0:T(8,128)(2,1)S(1)} %get-tuple-element.506), channel_id=1, source_target_pairs={{64,0},{68,4},{72,8},{76,12},{80,16},{84,20},{88,24},{92,28},{96,3... | collective-permute-start | bytes 786440 | tf_op jit(solution)/shard_map/ppermute | solution.py:16
  407.2 13.8 %collective-permute-start.17 = (bf16[128,1024]{1,0:T(8,128)(2,1)S(1)}, bf16[128,1024]{1,0:T(8,128)(2,1)S(1)}, u32[]{:S(2)}, u32[]{:S(2)}) collective-permute-start(bf16[128,1024]{1,0:T(8,128)(2,1)S(1)} %get-tuple-element.507), channel_id=1, source_target_pairs={{32,0},{36,4},{40,8},{44,12},{48,16},{52,20},{56,24},{60,28},{64,3... | collective-permute-start | bytes 786440 | tf_op jit(solution)/shard_map/ppermute | solution.py:16
  410.0 29.4 %collective-permute-start.16 = (bf16[128,1024]{1,0:T(8,128)(2,1)S(1)}, bf16[128,1024]{1,0:T(8,128)(2,1)S(1)}, u32[]{:S(2)}, u32[]{:S(2)}) collective-permute-start(bf16[128,1024]{1,0:T(8,128)(2,1)S(1)} %get-tuple-element.508), channel_id=1, source_target_pairs={{16,0},{20,4},{24,8},{28,12},{32,16},{36,20},{40,24},{44,28},{48,3... | collective-permute-start | bytes 786440 | tf_op jit(solution)/shard_map/ppermute | solution.py:16
  415.3 30.2 %collective-permute-start.15 = (bf16[128,1024]{1,0:T(8,128)(2,1)S(1)}, bf16[128,1024]{1,0:T(8,128)(2,1)S(1)}, u32[]{:S(2)}, u32[]{:S(2)}) collective-permute-start(bf16[128,1024]{1,0:T(8,128)(2,1)S(1)} %get-tuple-element.509), channel_id=1, source_target_pairs={{8,0},{12,4},{16,8},{20,12},{24,16},{28,20},{32,24},{36,28},{40,32... | collective-permute-start | bytes 786440 | tf_op jit(solution)/shard_map/ppermute | solution.py:16
